TPU v7x, 32 devices: a whole 2x2x4 slice. The times are simulated.
32 devices in a mesh: dp: 16 (over z, y, x), tensor: 2 (over core).
Axes of the slice: x: 2, y: 2, z: 4, core: 2. Of those that a mesh axis runs over, the one named last changes fastest.
Arguments:
- inputs: bfloat16 [2, 8192, 1024], P(None, ('dp', 'tensor')), may hold values from -6 to 6
- lengths: int32 [2, 16, 8], P(None, 'dp'), may hold values from 0 to 512, as said below
- query_weight: bfloat16 [1024, 1024], P(None, 'tensor'), may hold values from -0.1875 to 0.1875
- key_weight: bfloat16 [1024, 1024], P(None, 'tensor'), may hold values from -0.1875 to 0.1875
- value_weight: bfloat16 [1024, 1024], P(None, 'tensor'), may hold values from -0.1875 to 0.1875
- output_weight: bfloat16 [1024, 1024], P('tensor'), may hold values from -0.1875 to 0.1875
- inner_weight: bfloat16 [1024, 4096], P(None, 'tensor'), may hold values from -0.1875 to 0.1875
- outer_weight: bfloat16 [4096, 1024], P('tensor'), may hold values from -0.09375 to 0.09375
- entry_gain: float32 [1024], replicated, may hold values from 0.25 to 1.75
- entry_bias: float32 [1024], replicated, may hold values from -3 to 3
- merge_gain: float32 [1024], replicated, may hold values from 0.25 to 1.75
- merge_bias: float32 [1024], replicated, may hold values from -3 to 3
- inlet_gain: float32 [1024], replicated, may hold values from 0.25 to 1.75
- inlet_bias: float32 [1024], replicated, may hold values from -3 to 3
- outlet_gain: float32 [1024], replicated, may hold values from 0.25 to 1.75
- outlet_bias: float32 [1024], replicated, may hold values from -3 to 3
- cotangent: bfloat16 [2, 8192, 1024], P(None, ('dp', 'tensor')), may hold values from -6 to 6
Outputs:
- outputs: bfloat16 [2, 8192, 1024], P(None, ('dp', 'tensor'))
- input_grad: bfloat16 [2, 8192, 1024], P(None, ('dp', 'tensor'))
- query_grad: float32 [1024, 1024], P(None, 'tensor')
- key_grad: float32 [1024, 1024], P(None, 'tensor')
- value_grad: float32 [1024, 1024], P(None, 'tensor')
- output_grad: float32 [1024, 1024], P('tensor')
- inner_grad: float32 [1024, 4096], P(None, 'tensor')
- outer_grad: float32 [4096, 1024], P('tensor')
- gain_entry: float32 [1024], replicated
- bias_entry: float32 [1024], replicated
- gain_merge: float32 [1024], replicated
- bias_merge: float32 [1024], replicated
- gain_inlet: float32 [1024], replicated
- bias_inlet: float32 [1024], replicated
- gain_outlet: float32 [1024], replicated
- bias_outlet: float32 [1024], replicated
Inputs may be any that keep to these rules, and one draw needn't show every extreme that they name: `lengths`: each row lists the 8 sequences of one buffer packed in order from its first row; they sum to at most 512, the rest of the buffer is padding; slots may be empty; some buffer holds a single sequence of exactly 512.
All inputs are finite; a program needn't handle non-finite values.
Results may differ from a plain program's by a relative error of at most 0.015.
The roundings to bfloat16 on the way count: a program that leaves them out, or rounds other values in their place, can miss the bound.
Values may be sent and summed in bfloat16 or wider, within the bound.
No kernel may reach another device: no remote copies, remote signals or barrier semaphores. Data moves between devices by JAX's collectives and lax.ppermute only.
A program may use at most 192 MiB of HBM per device.

v0:
```python
import math
import jax
import jax.numpy as jnp
from jax import lax
from jax.sharding import PartitionSpec as P

HEAD = 64
NEGATIVE = -1e30


def layer_norm(values, gain, bias):
    center = values - jnp.mean(values, axis=-1, keepdims=True)
    spread = jnp.mean(center * center, axis=-1, keepdims=True)
    return center * lax.rsqrt(spread + 1e-05) * gain + bias


def exact_gelu(values):
    return jax.nn.gelu(values, approximate=False)


def seq_layout(lens, rows):
    ends = jnp.cumsum(lens, dtype=jnp.int32)
    index = jnp.arange(rows, dtype=jnp.int32)
    after = index[:, None] >= ends[None, :]
    segment = jnp.sum(after.astype(jnp.int32), axis=1)
    begin = jnp.max(jnp.where(after, ends[None, :], 0), axis=1)
    return (segment, (index - begin).astype(jnp.float32))


def rotary_tables(place, width):
    half = width // 2
    rate = jnp.exp(jnp.arange(half, dtype=jnp.float32) * (-math.log(10000.0) / half))
    angle = place[:, None] * rate[None, :]
    return (jnp.cos(angle)[:, None, :], jnp.sin(angle)[:, None, :])


def rotate(values, cosine, sine):
    half = values.shape[-1] // 2
    first = values[..., :half]
    second = values[..., half:]
    return jnp.concatenate(
        [first * cosine - second * sine, first * sine + second * cosine], axis=-1
    )


def rotate_back(grads, cosine, sine):
    half = grads.shape[-1] // 2
    first = grads[..., :half]
    second = grads[..., half:]
    return jnp.concatenate(
        [first * cosine + second * sine, second * cosine - first * sine], axis=-1
    )


def contract_rows(left, right):
    return lax.dot_general(
        left, right, (((0,), (0,)), ((), ())), preferred_element_type=jnp.float32
    )


def times_transpose(left, right):
    return lax.dot_general(
        left, right, (((1,), (1,)), ((), ())), preferred_element_type=jnp.float32
    )


def masked_scores(query_block, keys, segment, begin, block):
    rows = keys.shape[0]
    scores = (
        jnp.einsum("qhd,khd->hqk", query_block, keys, preferred_element_type=jnp.float32) * 0.125
    )
    query_index = begin + jnp.arange(block, dtype=jnp.int32)
    key_index = jnp.arange(rows, dtype=jnp.int32)
    allowed = (segment[:, None] == segment[None, :]) & (key_index[None, :] <= query_index[:, None])
    return jnp.where(allowed[None], scores, NEGATIVE)


def attend_forward(query, keys, values, segment, block):
    rows = keys.shape[0]

    def one_block(number):
        begin = number * block
        scores = masked_scores(query, keys, segment, begin, block)
        peak = jnp.max(scores, axis=-1, keepdims=True)
        raised = jnp.exp(scores - peak)
        total = jnp.sum(raised, axis=-1, keepdims=True)
        probs = (raised / total).astype(jnp.bfloat16)
        attended = jnp.einsum("hqk,khd->qhd", probs, values, preferred_element_type=jnp.float32)
        return (attended, (peak + jnp.log(total))[..., 0])

    attended, logsum = lax.map(one_block, jnp.arange(rows // block, dtype=jnp.int32))
    return (attended.reshape(rows, query.shape[1], query.shape[2]), logsum)


def attend_backward(query, keys, values, mixed_grad, segment, logsum, block):
    rows = keys.shape[0]

    def one_block(carry, packed):
        keys_acc, values_acc = carry
        number, block_logsum = packed
        begin = number * block
        scores = masked_scores(query, keys, segment, begin, block)
        probs = jnp.exp(scores - block_logsum[..., None])
        prob_grad = jnp.einsum(
            "qhd,khd->hqk", mixed_grad, values, preferred_element_type=jnp.float32
        )
        offset = jnp.sum(probs * prob_grad, axis=-1, keepdims=True)
        score_grad = (probs * (prob_grad - offset)).astype(jnp.bfloat16)
        query_part = (
            jnp.einsum("hqk,khd->qhd", score_grad, keys, preferred_element_type=jnp.float32) * 0.125
        )
        keys_acc = (
            keys_acc
            + jnp.einsum("hqk,qhd->khd", score_grad, query, preferred_element_type=jnp.float32)
            * 0.125
        )
        values_acc = values_acc + jnp.einsum(
            "hqk,qhd->khd",
            probs.astype(jnp.bfloat16),
            mixed_grad,
            preferred_element_type=jnp.float32,
        )
        return ((keys_acc, values_acc), query_part)

    empty = jnp.zeros(keys.shape, jnp.float32)
    numbers = jnp.arange(rows // block, dtype=jnp.int32)
    (keys_grad, values_grad), query_grad = lax.scan(one_block, (empty, empty), (numbers, logsum))
    return (query_grad.reshape(keys.shape), keys_grad, values_grad)


def on_device(
    inputs,
    lengths,
    query_weight,
    key_weight,
    value_weight,
    output_weight,
    inner_weight,
    outer_weight,
    entry_gain,
    entry_bias,
    merge_gain,
    merge_bias,
    inlet_gain,
    inlet_bias,
    outlet_gain,
    outlet_bias,
    cotangent,
):
    groups = lax.axis_size("tensor")
    local_rows = inputs.shape[1]
    rows = local_rows * groups
    width = query_weight.shape[1]
    block = min(512, rows)
    joined = jnp.concatenate([query_weight, key_weight, value_weight], axis=1)
    inner_use, outer_use = (inner_weight, outer_weight)
    joined_acc = jnp.zeros(joined.shape, jnp.float32)
    output_acc = jnp.zeros(output_weight.shape, jnp.float32)
    inner_acc = jnp.zeros(inner_use.shape, jnp.float32)
    outer_acc = jnp.zeros(outer_use.shape, jnp.float32)
    norm_acc = [jnp.zeros(entry_gain.shape, jnp.float32) for index in range(8)]
    result_list = []
    grad_list = []
    for micro in range(inputs.shape[0]):
        segment, place = seq_layout(lengths[micro, 0], rows)
        cosine, sine = rotary_tables(place, HEAD)
        resid = inputs[micro].astype(jnp.float32)
        normed, entry_pull = jax.vjp(layer_norm, resid, entry_gain, entry_bias)
        gathered = lax.all_gather(normed.astype(jnp.bfloat16), "tensor", axis=0, tiled=True)
        projected = jnp.dot(gathered, joined, preferred_element_type=jnp.float32)
        query = rotate(
            projected[:, :width].reshape(rows, width // HEAD, HEAD), cosine, sine
        ).astype(jnp.bfloat16)
        keys = rotate(
            projected[:, width : 2 * width].reshape(rows, width // HEAD, HEAD), cosine, sine
        ).astype(jnp.bfloat16)
        values = projected[:, 2 * width :].reshape(rows, width // HEAD, HEAD).astype(jnp.bfloat16)
        attended, logsum = attend_forward(query, keys, values, segment, block)
        mixed = attended.reshape(rows, width).astype(jnp.bfloat16)
        branch = lax.psum_scatter(
            jnp.dot(mixed, output_weight, preferred_element_type=jnp.float32),
            "tensor",
            scatter_dimension=0,
            tiled=True,
        )
        merged, merge_pull = jax.vjp(layer_norm, branch, merge_gain, merge_bias)
        hidden = resid + merged
        inlet, inlet_pull = jax.vjp(layer_norm, hidden, inlet_gain, inlet_bias)
        inlet_low = inlet.astype(jnp.bfloat16)
        feed = lax.all_gather(inlet_low, "tensor", axis=0, tiled=True)
        pre_act = jnp.dot(feed, inner_use, preferred_element_type=jnp.float32)
        activated, gelu_pull = jax.vjp(exact_gelu, pre_act)
        act_low = activated.astype(jnp.bfloat16)
        second = lax.psum_scatter(
            jnp.dot(act_low, outer_use, preferred_element_type=jnp.float32),
            "tensor",
            scatter_dimension=0,
            tiled=True,
        )
        finished, outlet_pull = jax.vjp(layer_norm, second, outlet_gain, outlet_bias)
        result_list.append((hidden + finished).astype(jnp.bfloat16))
        upstream = cotangent[micro].astype(jnp.float32)
        second_grad, outlet_gain_part, outlet_bias_part = outlet_pull(upstream)
        second_low = second_grad.astype(jnp.bfloat16)
        back_feed = lax.all_gather(second_low, "tensor", axis=0, tiled=True)
        outer_term = contract_rows(act_low, back_feed)
        act_grad = times_transpose(back_feed, outer_use)
        (pre_grad,) = gelu_pull(act_grad)
        pre_low = pre_grad.astype(jnp.bfloat16)
        inner_term = contract_rows(feed, pre_low)
        inlet_grad = lax.psum_scatter(
            times_transpose(pre_low, inner_use), "tensor", scatter_dimension=0, tiled=True
        )
        hidden_part, inlet_gain_part, inlet_bias_part = inlet_pull(inlet_grad)
        hidden_grad = upstream + hidden_part
        branch_grad, merge_gain_part, merge_bias_part = merge_pull(hidden_grad)
        back_mix = lax.all_gather(branch_grad.astype(jnp.bfloat16), "tensor", axis=0, tiled=True)
        output_term = contract_rows(mixed, back_mix)
        mixed_grad = (
            times_transpose(back_mix, output_weight)
            .astype(jnp.bfloat16)
            .reshape(rows, width // HEAD, HEAD)
        )
        query_part, keys_part, values_part = attend_backward(
            query, keys, values, mixed_grad, segment, logsum, block
        )
        projected_grad = jnp.concatenate(
            [
                rotate_back(query_part, cosine, sine).reshape(rows, width),
                rotate_back(keys_part, cosine, sine).reshape(rows, width),
                values_part.reshape(rows, width),
            ],
            axis=1,
        ).astype(jnp.bfloat16)
        joined_term = contract_rows(gathered, projected_grad)
        normed_grad = lax.psum_scatter(
            times_transpose(projected_grad, joined).astype(jnp.bfloat16),
            "tensor",
            scatter_dimension=0,
            tiled=True,
        ).astype(jnp.float32)
        resid_part, entry_gain_part, entry_bias_part = entry_pull(normed_grad)
        grad_list.append((hidden_grad + resid_part).astype(jnp.bfloat16))
        parts = [
            entry_gain_part,
            entry_bias_part,
            merge_gain_part,
            merge_bias_part,
            inlet_gain_part,
            inlet_bias_part,
            outlet_gain_part,
            outlet_bias_part,
        ]
        norm_acc = [total + piece for total, piece in zip(norm_acc, parts)]
        joined_acc = joined_acc + joined_term
        output_acc = output_acc + output_term
        inner_acc = inner_acc + inner_term
        outer_acc = outer_acc + outer_term
    joined_acc, output_acc, inner_acc, outer_acc = lax.psum(
        (joined_acc, output_acc, inner_acc, outer_acc), "dp"
    )
    norm_sums = lax.psum(
        (
            norm_acc[0],
            norm_acc[1],
            norm_acc[2],
            norm_acc[3],
            norm_acc[4],
            norm_acc[5],
            norm_acc[6],
            norm_acc[7],
        ),
        ("dp", "tensor"),
    )
    return (
        jnp.stack(result_list),
        jnp.stack(grad_list),
        joined_acc[:, :width],
        joined_acc[:, width : 2 * width],
        joined_acc[:, 2 * width :],
        output_acc,
        inner_acc,
        outer_acc,
        norm_sums[0],
        norm_sums[1],
        norm_sums[2],
        norm_sums[3],
        norm_sums[4],
        norm_sums[5],
        norm_sums[6],
        norm_sums[7],
    )


def solution(mesh):
    placed = (
        P(None, ("dp", "tensor"), None),
        P(None, "dp", None),
        P(None, "tensor"),
        P(None, "tensor"),
        P(None, "tensor"),
        P("tensor", None),
        P(None, "tensor"),
        P("tensor", None),
        P(),
        P(),
        P(),
        P(),
        P(),
        P(),
        P(),
        P(),
        P(None, ("dp", "tensor"), None),
    )
    return jax.shard_map(
        on_device,
        mesh=mesh,
        in_specs=placed,
        out_specs=(
            P(None, ("dp", "tensor"), None),
            P(None, ("dp", "tensor"), None),
            P(None, "tensor"),
            P(None, "tensor"),
            P(None, "tensor"),
            P("tensor", None),
            P(None, "tensor"),
            P("tensor", None),
            P(),
            P(),
            P(),
            P(),
            P(),
            P(),
            P(),
            P(),
        ),
        check_vma=False,
    )
```

profile of v0, /device:TPU:0, one launch (start us, length us, event | category | flops | bytes accessed | tf_op | source)
XLA Modules:
  0.0 979.6 jit_solution(8197130521890826717)
XLA Ops:
  7.3 1.6 convert_reduce_fusion.5
  8.9 1.6 fusion.68
  11.1 2.6 fusion.65
  18.9 2.3 constant_dynamic-update-slice_fusion
  21.8 3.9 all-gather.13.cloned.1.call-done
  25.8 4.0 fusion.125
  32.1 1.6 copy.71
  33.7 2.1 copy.69
  36.1 2.7 fusion.121
  40.1 2.2 copy-done.2
  42.3 1.6 fusion.46
  44.7 2.1 fusion.126
  47.3 4.0 fusion.122
  53.6 1.7 copy.67
  55.3 2.1 copy.65
  57.7 1.6 fusion.120
  60.5 2.2 copy-done.1
  62.7 1.6 fusion.47
  65.1 2.1 fusion.123
  70.1 8.1 reduce-scatter.9.cloned.1.call-done
  79.6 1.5 multiply_reduce_fusion.15
  81.1 2.2 fusion.112
  86.6 9.5 all-gather.15.cloned.1.call-done
  96.1 15.0 %multiply_convert_fusion.2 = (bf16[512,2048]{1,0:T(8,128)(2,1)S(1)}, f32[512,2048]{1,0:T(8,128)}, f32[512,2048]{1,0:T(8,128)}) fusion(bf16[512,1024]{1,0:T(8,128)(2,1)} %all-gather.15.cloned.1.call-done, bf16[1024,2048]{1,0:T(8,128)(2,1)} %param.23), kind=kOutput, calls=%fused_computation.27 | convolution fusion | flops 2215641088 | bytes 15728640 | tf_op jit(solution)/shard_map/dot_general | solution.py:191
  112.5 3.6 fusion.127
  116.6 14.9 %multiply_convert_fusion.3 = (bf16[512,2048]{1,0:T(8,128)(2,1)S(1)}, f32[512,2048]{1,0:T(8,128)}, f32[512,2048]{1,0:T(8,128)}) fusion(bf16[512,1024]{1,0:T(8,128)(2,1)} %all-gather.11.cloned.1.call-done, bf16[1024,2048]{1,0:T(8,128)(2,1)} %param.23), kind=kOutput, calls=%fused_computation.40 | convolution fusion | flops 2215641088 | bytes 15728640 | tf_op jit(solution)/shard_map/dot_general | solution.py:191
  132.8 3.6 fusion.124
  139.5 7.9 reduce-scatter.11.cloned.1.call-done
  148.8 1.6 multiply_reduce_fusion.13
  150.5 2.7 fusion.72
  153.2 2.1 fusion.110
  156.3 2.1 add_convert_fusion.7
  158.7 7.9 all-gather.21.cloned.1.call-done
  166.6 8.5 add_convert_fusion
  176.5 3.7 fusion.129
  180.3 8.5 add_convert_fusion.1
  190.2 3.7 fusion.128
  194.2 7.5 fusion.132
  201.7 4.4 reduce-scatter.17.cloned.1.call-done
  206.0 2.4 multiply_reduce_fusion.3
  211.4 1.6 fusion.103
  214.1 9.5 convolution_add_fusion.1
  223.7 5.7 fusion.131
  230.8 2.0 convolution_convert_fusion.2
  232.9 5.4 multiply_reduce_fusion
  238.9 2.5 multiply_convert_fusion
  246.5 2.8 convolution_convert_fusion
  249.6 2.0 convolution_convert_fusion.3
  251.6 5.4 multiply_reduce_fusion.1
  257.7 2.5 multiply_convert_fusion.1
  265.3 2.8 convolution_convert_fusion.1
  268.4 9.9 %convolution_add_fusion.2 = f32[1024,2048]{1,0:T(8,128)} fusion(f32[1024,2048]{1,0:T(8,128)} %fusion.131, bf16[512,1024]{1,0:T(8,128)(2,1)S(1)} %copy-done.22, bf16[512,2048]{1,0:T(8,128)(2,1)} %copy-done.23), kind=kOutput, calls=%fused_computation.58 | convolution fusion | flops 2149580800 | bytes 19922944 | tf_op jit(solution)/shard_map/dot_general | solution.py:56
  279.6 2.1 convolution_add_fusion.3
  281.7 1.9 fusion.80
  283.6 4.6 convolution_add_fusion
  289.7 2.4 pad_maximum_fusion.2
  292.1 1.8 fusion.69
  294.0 2.6 fusion.74
  296.6 45.4 %all-reduce = (f32[1024]{0:T(1024)}, f32[1024]{0:T(1024)}, f32[1024]{0:T(1024)}, f32[1024]{0:T(1024)}, f32[1024]{0:T(1024)}, /*index=5*/f32[1024]{0:T(1024)}, f32[1024]{0:T(1024)}, f32[1024]{0:T(1024)}) all-reduce(f32[1024]{0:T(1024)S(1)} %add.355, f32[1024]{0:T(1024)S(1)} %add.356, ...), channel_id=1, replica_groups=mesh['dp'=16,'tensor'=2] {'dp','tensor'}, use_global_device_ids=true, to_apply=%region_58.59 | all-reduce | flops 8192 | bytes 65536 | tf_op jit(solution)/shard_map/psum | solution.py:262
  342.1 2.5 fusion.83
  345.6 609.3 %all-reduce.4.cloned.1.call-done = (f32[1024,1536]{1,0:T(8,128)}, f32[512,1024]{1,0:T(8,128)}, f32[1024,2048]{1,0:T(8,128)}, f32[2048,1024]{1,0:T(8,128)}) async-done(((f32[1024,1536]{1,0:T(8,128)}, f32[512,1024]{1,0:T(8,128)}, f32[1024,2048]{1,0:T(8,128)}, f32[2048,1024]{1,0:T(8,128)}), (f32[1024,1536]{1,0:T(8,128)}, f32[512,1024]{1,0:T(8,128)}, f32[1024,2048]{1,0:T(8,128)}, ...) | async-done | bytes 25165840 | tf_op jit(solution)/shard_map/psum | solution.py:259
  954.9 6.3 fusion.117
  963.8 4.3 copy.94
  969.5 3.4 copy.95
  (367 shorter events, 60.1 us)
Async XLA Ops:
  7.2 37.5 %copy-start = (bf16[512,1024]{1,0:T(8,128)(2,1)S(1)}, bf16[512,1024]{1,0:T(8,128)(2,1)}, u32[]{:S(2)}) copy-start(bf16[512,1024]{1,0:T(8,128)(2,1)} %param.22) | copy-start | bytes 3145732
  7.2 7.4 copy-start.55
  7.2 8.5 copy-start.96
  7.2 10.6 %copy-start.56 = (bf16[1024,512]{1,0:T(8,128)(2,1)S(1)}, bf16[1024,512]{1,0:T(8,128)(2,1)}, u32[]{:S(2)}) copy-start(bf16[1024,512]{1,0:T(8,128)(2,1)} %param.20) | copy-start | bytes 3145732
  7.2 18.5 %all-gather.13.cloned.1.call-start = ((), (), s32[]{:S(2)}) async-start(), calls=%async_computation.12 | async-start | bytes 1572864 | tf_op jit(solution)/shard_map/all_gather | solution.py:169
  8.9 4.9 copy-start.79
  13.8 33.5 %all-gather.9.cloned.1.call-start = ((), (), s32[]{:S(2)}) async-start(), calls=%async_computation.8 | async-start | bytes 1572864 | tf_op jit(solution)/shard_map/all_gather | solution.py:169
  14.5 52.7 %reduce-scatter.13.cloned.1.call-start = ((), (), s32[]{:S(2)}) async-start(), calls=%async_computation.13 | async-start | bytes 3145728 | tf_op jit(solution)/shard_map/reduce_scatter | solution.py:180
  21.8 13.9 %copy-start.62 = (f32[512,32]{0,1:T(8,128)}, f32[512,32]{0,1:T(8,128)S(1)}, u32[]{:S(2)}) copy-start(f32[512,32]{0,1:T(8,128)S(1)} %get-tuple-element.251) | copy-start | bytes 196612
  21.8 13.9 %copy-start.64 = (f32[512,32]{0,1:T(8,128)}, f32[512,32]{0,1:T(8,128)S(1)}, u32[]{:S(2)}) copy-start(f32[512,32]{0,1:T(8,128)S(1)} %get-tuple-element.252) | copy-start | bytes 196612
  21.8 35.5 %copy-start.58 = (f32[512,32]{0,1:T(8,128)}, f32[512,32]{0,1:T(8,128)S(1)}, u32[]{:S(2)}) copy-start(f32[512,32]{0,1:T(8,128)S(1)} %get-tuple-element.245) | copy-start | bytes 196612
  21.8 35.5 %copy-start.60 = (f32[512,32]{0,1:T(8,128)}, f32[512,32]{0,1:T(8,128)S(1)}, u32[]{:S(2)}) copy-start(f32[512,32]{0,1:T(8,128)S(1)} %get-tuple-element.246) | copy-start | bytes 196612
  46.8 31.4 %reduce-scatter.9.cloned.1.call-start = ((), (), s32[]{:S(2)}) async-start(), calls=%async_computation.9 | async-start | bytes 3145728 | tf_op jit(solution)/shard_map/reduce_scatter | solution.py:180
  65.1 16.0 %copy-start.3 = (bf16[2,256,1024]{2,1,0:T(8,128)(2,1)S(1)}, bf16[2,256,1024]{2,1,0:T(8,128)(2,1)}, u32[]{:S(2)}) copy-start(bf16[2,256,1024]{2,1,0:T(8,128)(2,1)} %param.17) | copy-start | bytes 3145732
  65.1 16.0 %copy-start.82 = (f32[1024]{0:T(1024)S(1)}, f32[1024]{0:T(1024)}, u32[]{:S(2)}) copy-start(f32[1024]{0:T(1024)} %param.27) | copy-start | bytes 12292
  65.1 16.0 %copy-start.95 = (f32[1024]{0:T(1024)S(1)}, f32[1024]{0:T(1024)}, u32[]{:S(2)}) copy-start(f32[1024]{0:T(1024)} %param.28) | copy-start | bytes 12292
  67.2 28.9 %all-gather.15.cloned.1.call-start = ((), (), s32[]{:S(2)}) async-start(), calls=%async_computation.14 | async-start | bytes 1572864 | tf_op jit(solution)/shard_map/all_gather | solution.py:190
  79.6 4.8 copy-start.81
  79.6 4.8 copy-start.93
  85.7 30.9 %all-gather.11.cloned.1.call-start = ((), (), s32[]{:S(2)}) async-start(), calls=%async_computation.10 | async-start | bytes 1572864 | tf_op jit(solution)/shard_map/all_gather | solution.py:190
  86.3 50.3 %reduce-scatter.15.cloned.1.call-start = ((), (), s32[]{:S(2)}) async-start(), calls=%async_computation.15 | async-start | bytes 3145728 | tf_op jit(solution)/shard_map/reduce_scatter | solution.py:194
  96.1 16.3 %copy-start.97 = (bf16[2048,1024]{1,0:T(8,128)(2,1)S(1)}, bf16[2048,1024]{1,0:T(8,128)(2,1)}, u32[]{:S(2)}) copy-start(bf16[2048,1024]{1,0:T(8,128)(2,1)} %param.24) | copy-start | bytes 12582916
  116.1 31.3 %reduce-scatter.11.cloned.1.call-start = ((), (), s32[]{:S(2)}) async-start(), calls=%async_computation.11 | async-start | bytes 3145728 | tf_op jit(solution)/shard_map/reduce_scatter | solution.py:194
  116.6 16.2 %copy-start.98 = (bf16[2048,1024]{1,0:T(8,128)(2,1)S(1)}, bf16[2048,1024]{1,0:T(8,128)(2,1)}, u32[]{:S(2)}) copy-start(bf16[2048,1024]{1,0:T(8,128)(2,1)} %param.24) | copy-start | bytes 12582916
  136.5 14.0 %copy-start.84 = (f32[1024]{0:T(1024)S(1)}, f32[1024]{0:T(1024)}, u32[]{:S(2)}) copy-start(f32[1024]{0:T(1024)} %param.31) | copy-start | bytes 12292
  136.5 16.7 %copy-start.6 = (f32[256,1024]{1,0:T(8,128)S(1)}, f32[256,1024]{1,0:T(8,128)}, u32[]{:S(2)}) copy-start(f32[256,1024]{1,0:T(8,128)} %copy-done.5) | copy-start | bytes 3145732
  136.5 16.7 %copy-start.94 = (f32[1024]{0:T(1024)S(1)}, f32[1024]{0:T(1024)}, u32[]{:S(2)}) copy-start(f32[1024]{0:T(1024)} %param.32) | copy-start | bytes 12292
  136.5 30.1 %all-gather.21.cloned.1.call-start = ((), (), s32[]{:S(2)}) async-start(), calls=%async_computation.20 | async-start | bytes 1572864 | tf_op jit(solution)/shard_map/all_gather | solution.py:205
  148.8 4.4 copy-start.9
  148.8 4.4 copy-start.10
  148.8 4.4 copy-start.11
  156.3 24.0 %all-gather.17.cloned.1.call-start = ((), (), s32[]{:S(2)}) async-start(), calls=%async_computation.16 | async-start | bytes 1572864 | tf_op jit(solution)/shard_map/all_gather | solution.py:205
  158.5 43.2 %reduce-scatter.21.cloned.1.call-start = ((), (), s32[]{:S(2)}) async-start(), calls=%async_computation.21 | async-start | bytes 3145728 | tf_op jit(solution)/shard_map/reduce_scatter | solution.py:211
  166.6 9.9 %copy-start.99 = (bf16[1024,2048]{1,0:T(8,128)(2,1)S(1)}, bf16[1024,2048]{1,0:T(8,128)(2,1)}, u32[]{:S(2)}) copy-start(bf16[1024,2048]{1,0:T(8,128)(2,1)} %param.23) | copy-start | bytes 12582916
  180.2 25.8 %reduce-scatter.17.cloned.1.call-start = ((), (), s32[]{:S(2)}) async-start(), calls=%async_computation.17 | async-start | bytes 3145728 | tf_op jit(solution)/shard_map/reduce_scatter | solution.py:211
  180.3 9.9 %copy-start.100 = (bf16[1024,2048]{1,0:T(8,128)(2,1)S(1)}, bf16[1024,2048]{1,0:T(8,128)(2,1)}, u32[]{:S(2)}) copy-start(bf16[1024,2048]{1,0:T(8,128)(2,1)} %param.23) | copy-start | bytes 12582916
  190.2 4.0 copy-start.75
  193.9 37.0 %all-gather.23.cloned.1.call-start = ((), (), s32[]{:S(2)}) async-start(), calls=%async_computation.22 | async-start | bytes 1572864 | tf_op jit(solution)/shard_map/all_gather | solution.py:217
  214.0 35.5 %all-gather.19.cloned.1.call-start = ((), (), s32[]{:S(2)}) async-start(), calls=%async_computation.18 | async-start | bytes 1572864 | tf_op jit(solution)/shard_map/all_gather | solution.py:217
  214.1 9.6 copy-start.102
  214.1 9.6 copy-start.105
  223.7 5.7 copy-start.19
  230.4 61.7 %reduce-scatter.23.cloned.1.call-start = ((), (), s32[]{:S(2)}) async-start(), calls=%async_computation.23 | async-start | bytes 1572864 | tf_op jit(solution)/shard_map/reduce_scatter | solution.py:236
  232.8 5.5 slice-start.2
  232.8 6.1 slice-start.3
  249.3 42.8 %reduce-scatter.19.cloned.1.call-start = ((), (), s32[]{:S(2)}) async-start(), calls=%async_computation.19 | async-start | bytes 1572864 | tf_op jit(solution)/shard_map/reduce_scatter | solution.py:236
  251.5 5.5 slice-start
  251.5 6.2 slice-start.1
  268.1 10.2 %copy-start.25 = (bf16[8,64,512]{2,1,0:T(8,128)(2,1)S(1)}, bf16[8,64,512]{2,1,0:T(8,128)(2,1)}, u32[]{:S(2)}) copy-start(bf16[8,64,512]{2,1,0:T(8,128)(2,1)} %copy-done.24) | copy-start | bytes 1572868
  268.2 686.7 %all-reduce.4.cloned.1.call-start = ((), (), s32[]{:S(2)}) async-start(), calls=%async_computation.24 | async-start | bytes 50331648 | tf_op jit(solution)/shard_map/psum | solution.py:259
  268.4 9.9 %copy-start.38 = (bf16[512,1024]{1,0:T(8,128)(2,1)S(1)}, bf16[512,1024]{1,0:T(8,128)(2,1)}, u32[]{:S(2)}) copy-start(bf16[512,1024]{1,0:T(8,128)(2,1)} %all-gather.19.cloned.1.call-done) | copy-start | bytes 3145732
  268.4 10.7 %copy-start.36 = (bf16[8,64,512]{2,1,0:T(8,128)(2,1)S(1)}, bf16[8,64,512]{2,1,0:T(8,128)(2,1)}, u32[]{:S(2)}) copy-start(bf16[8,64,512]{2,1,0:T(8,128)(2,1)} %copy-done.35) | copy-start | bytes 1572868
  288.2 3.9 copy-start.78
  288.2 3.9 copy-start.80
  289.4 4.5 copy-start.92
  289.4 4.6 copy-start.90
  289.4 4.6 copy-start.86
  289.4 4.6 copy-start.88
  289.6 52.5 %copy-start.15 = (f32[256,1024]{1,0:T(8,128)S(1)}, f32[256,1024]{1,0:T(8,128)}, u32[]{:S(2)}) copy-start(f32[256,1024]{1,0:T(8,128)} %copy-done.14) | copy-start | bytes 3145732
  954.9 7.7 slice-start.6
  954.9 6.3 copy-start.34
  954.9 8.9 slice-start.7
  961.2 6.9 slice-start.4
  963.8 5.6 slice-start.5
  (67 other events, 141.3 us)
Sparse Core Ops, SparseCore 0:
  13.9 11.8 all-gather.12
  27.9 10.1 all-gather.8
  46.9 10.6 reduce-scatter.12
  67.3 10.8 reduce-scatter.8
  85.9 10.2 all-gather.14
  98.1 10.1 all-gather.10
  116.2 10.7 reduce-scatter.14
  136.6 10.7 reduce-scatter.10
  156.4 10.2 all-gather.20
  168.6 10.1 all-gather.16
  181.7 10.7 reduce-scatter.20
  195.2 10.7 reduce-scatter.16
  214.2 10.2 all-gather.22
  230.5 10.2 all-gather.18
  249.4 9.7 reduce-scatter.22
  268.3 9.7 reduce-scatter.18
  288.4 666.4 all-reduce.3
where the time goes:
time: 988 us; the launch traced here: 980 us
  waiting for transfers between devices  653 us (66%)
  matrix products  151 us (15%)
  other arithmetic  59.3 us (6%)
  local copies, waits for them, and re-layouts  53.1 us (5%)
  blocking collectives  45.4 us (5%)
  between operations  15.9 us (2%)
    psum x1, waiting for transfers between devices, on_device(): lax.psum((joined_acc, output_acc, inner_acc, outer_acc), 'dp')  609 us
    psum x1, blocking collectives, on_device(): lax.psum((norm_acc[0], norm_acc[1], norm_acc[2], norm_acc[3], norm_acc[4]...  45.4 us
    dot_general x8, matrix products, contract_rows(): lax.dot_general(left, right, (((0,), (0,)), ((), ())), preferred_element_...  41.9 us
    dot_general x8, matrix products, times_transpose(): lax.dot_general(left, right, (((1,), (1,)), ((), ())), preferred_element_...  34 us
    unnamed x233, local copies, waits for them, and re-layouts  32.4 us
    dot_general x2, matrix products, on_device(): pre_act = jnp.dot(feed, inner_use, preferred_element_type=jnp.float32)  29.8 us
  transfers between devices with their start and end apart: 17, of which 7 were waited for; matrix products, arithmetic and copies ran while one was open for 20% of the time, Pallas kernels for 0%

commit v1 on v0

--- a/solution.py
+++ b/solution.py
@@ -259,19 +259,17 @@
     joined_acc, output_acc, inner_acc, outer_acc = lax.psum(
         (joined_acc, output_acc, inner_acc, outer_acc), "dp"
     )
-    norm_sums = lax.psum(
-        (
-            norm_acc[0],
-            norm_acc[1],
-            norm_acc[2],
-            norm_acc[3],
-            norm_acc[4],
-            norm_acc[5],
-            norm_acc[6],
-            norm_acc[7],
-        ),
-        ("dp", "tensor"),
-    )
+    work_x = (
+        norm_acc[0],
+        norm_acc[1],
+        norm_acc[2],
+        norm_acc[3],
+        norm_acc[4],
+        norm_acc[5],
+        norm_acc[6],
+        norm_acc[7],
+    )
+    norm_sums = lax.psum(lax.psum(work_x, "tensor"), axis_name="dp")
     return (
         jnp.stack(result_list),
         jnp.stack(grad_list),

time: 988 us -> 988 us (level)
  waiting for transfers between devices: 653 us -> 612 us
  blocking collectives: 45.4 us -> 85.6 us
    psum x1, waiting for transfers between devices: 609 us -> 569 us  [on_device(): lax.psum((joined_acc, output_acc, inner_acc, outer_acc), 'dp')]
    psum x1 -> x2, blocking collectives: 45.4 us -> 85.6 us  [on_device(): norm_sums = lax.psum(lax.psum(work_x, 'tensor'), axis_name='dp')]
where the time goes in v1:
time: 988 us; the launch traced here: 979 us
  waiting for transfers between devices  612 us (62%)
  matrix products  150 us (15%)
  blocking collectives  85.6 us (9%)
  other arithmetic  59.4 us (6%)
  local copies, waits for them, and re-layouts  53.1 us (5%)
  between operations  15.9 us (2%)
    psum x1, waiting for transfers between devices, on_device(): lax.psum((joined_acc, output_acc, inner_acc, outer_acc), 'dp')  569 us
    psum x2, blocking collectives, on_device(): norm_sums = lax.psum(lax.psum(work_x, 'tensor'), axis_name='dp')  85.6 us
    dot_general x8, matrix products, contract_rows(): lax.dot_general(left, right, (((0,), (0,)), ((), ())), preferred_element_...  41.9 us
    dot_general x8, matrix products, times_transpose(): lax.dot_general(left, right, (((1,), (1,)), ((), ())), preferred_element_...  34 us
    unnamed x233, local copies, waits for them, and re-layouts  32.3 us
    dot_general x2, matrix products, on_device(): pre_act = jnp.dot(feed, inner_use, preferred_element_type=jnp.float32)  29.7 us
  transfers between devices with their start and end apart: 17, of which 7 were waited for; matrix products, arithmetic and copies ran while one was open for 20% of the time, Pallas kernels for 0%

profile of v1, /device:TPU:0, one launch (start us, length us, event | category | flops | bytes accessed | tf_op | source)
XLA Modules:
  0.0 979.4 jit_solution(17474209392059507621)
XLA Ops:
  7.3 1.6 convert_reduce_fusion.5
  8.9 1.6 fusion.68
  11.1 2.6 fusion.65
  18.9 2.4 constant_dynamic-update-slice_fusion
  21.8 3.9 all-gather.13.cloned.1.call-done
  25.8 4.0 fusion.125
  32.1 1.6 copy.71
  33.7 2.1 copy.69
  36.1 2.7 fusion.121
  40.1 2.2 copy-done.2
  42.3 1.6 fusion.46
  44.7 2.1 fusion.126
  47.2 4.0 fusion.122
  53.6 1.7 copy.67
  55.3 2.1 copy.65
  57.7 1.6 fusion.120
  60.5 2.2 copy-done.1
  62.7 1.6 fusion.47
  65.1 2.1 fusion.123
  70.1 8.1 reduce-scatter.9.cloned.1.call-done
  81.1 2.2 fusion.112
  86.6 9.5 all-gather.15.cloned.1.call-done
  96.1 14.9 %multiply_convert_fusion.2 = (bf16[512,2048]{1,0:T(8,128)(2,1)S(1)}, f32[512,2048]{1,0:T(8,128)}, f32[512,2048]{1,0:T(8,128)}) fusion(bf16[512,1024]{1,0:T(8,128)(2,1)} %all-gather.15.cloned.1.call-done, bf16[1024,2048]{1,0:T(8,128)(2,1)} %param.23), kind=kOutput, calls=%fused_computation.27 | convolution fusion | flops 2215641088 | bytes 15728640 | tf_op jit(solution)/shard_map/dot_general | solution.py:191
  112.4 3.6 fusion.127
  116.5 14.8 %multiply_convert_fusion.3 = (bf16[512,2048]{1,0:T(8,128)(2,1)S(1)}, f32[512,2048]{1,0:T(8,128)}, f32[512,2048]{1,0:T(8,128)}) fusion(bf16[512,1024]{1,0:T(8,128)(2,1)} %all-gather.11.cloned.1.call-done, bf16[1024,2048]{1,0:T(8,128)(2,1)} %param.23), kind=kOutput, calls=%fused_computation.40 | convolution fusion | flops 2215641088 | bytes 15728640 | tf_op jit(solution)/shard_map/dot_general | solution.py:191
  132.7 3.6 fusion.124
  139.4 7.9 reduce-scatter.11.cloned.1.call-done
  148.7 1.6 multiply_reduce_fusion.13
  150.3 2.7 fusion.72
  153.1 2.1 fusion.110
  156.2 2.1 add_convert_fusion.7
  158.6 7.9 all-gather.21.cloned.1.call-done
  166.5 8.5 add_convert_fusion
  176.3 3.7 fusion.129
  180.1 8.5 add_convert_fusion.1
  190.0 3.7 fusion.128
  194.0 7.5 fusion.132
  201.5 4.4 reduce-scatter.17.cloned.1.call-done
  205.9 2.4 multiply_reduce_fusion.3
  211.3 1.6 fusion.103
  214.0 9.5 convolution_add_fusion.1
  223.5 5.7 fusion.131
  230.7 2.0 convolution_convert_fusion.2
  232.7 5.4 multiply_reduce_fusion
  238.7 2.5 multiply_convert_fusion
  246.3 2.8 convolution_convert_fusion
  249.4 2.0 convolution_convert_fusion.3
  251.4 5.4 multiply_reduce_fusion.1
  257.6 2.5 multiply_convert_fusion.1
  265.1 2.8 convolution_convert_fusion.1
  268.3 9.9 %convolution_add_fusion.2 = f32[1024,2048]{1,0:T(8,128)} fusion(f32[1024,2048]{1,0:T(8,128)} %fusion.131, bf16[512,1024]{1,0:T(8,128)(2,1)S(1)} %copy-done.22, bf16[512,2048]{1,0:T(8,128)(2,1)} %copy-done.23), kind=kOutput, calls=%fused_computation.58 | convolution fusion | flops 2149580800 | bytes 19922944 | tf_op jit(solution)/shard_map/dot_general | solution.py:56
  279.4 2.1 convolution_add_fusion.3
  281.5 1.9 fusion.80
  283.4 4.6 convolution_add_fusion
  289.5 2.4 pad_maximum_fusion.2
  292.0 1.8 fusion.69
  293.8 2.6 fusion.74
  296.4 3.5 all-reduce.2
  299.9 82.2 %all-reduce = (f32[1024]{0:T(1024)}, f32[1024]{0:T(1024)}, f32[1024]{0:T(1024)}, f32[1024]{0:T(1024)}, f32[1024]{0:T(1024)}, /*index=5*/f32[1024]{0:T(1024)}, f32[1024]{0:T(1024)}, f32[1024]{0:T(1024)}) all-reduce(f32[1024]{0:T(1024)S(1)} %get-tuple-element.168, ...), channel_id=1, replica_groups=mesh['dp'=16,'tensor'=2] {'dp'}, use_global_device_ids=true, to_apply=%region_59.60 | all-reduce | flops 8192 | bytes 65536 | tf_op jit(solution)/shard_map/psum | solution.py:272
  382.1 2.5 fusion.83
  385.7 569.0 %all-reduce.5.cloned.1.call-done = (f32[1024,1536]{1,0:T(8,128)}, f32[512,1024]{1,0:T(8,128)}, f32[1024,2048]{1,0:T(8,128)}, f32[2048,1024]{1,0:T(8,128)}) async-done(((f32[1024,1536]{1,0:T(8,128)}, f32[512,1024]{1,0:T(8,128)}, f32[1024,2048]{1,0:T(8,128)}, f32[2048,1024]{1,0:T(8,128)}), (f32[1024,1536]{1,0:T(8,128)}, f32[512,1024]{1,0:T(8,128)}, f32[1024,2048]{1,0:T(8,128)}, ...) | async-done | bytes 25165840 | tf_op jit(solution)/shard_map/psum | solution.py:259
  954.7 6.3 fusion.117
  963.6 4.3 copy.94
  969.3 3.4 copy.95
  (368 shorter events, 61.6 us)
Async XLA Ops:
  7.2 37.5 %copy-start = (bf16[512,1024]{1,0:T(8,128)(2,1)S(1)}, bf16[512,1024]{1,0:T(8,128)(2,1)}, u32[]{:S(2)}) copy-start(bf16[512,1024]{1,0:T(8,128)(2,1)} %param.22) | copy-start | bytes 3145732
  7.2 7.4 copy-start.55
  7.2 8.5 copy-start.96
  7.2 10.6 %copy-start.56 = (bf16[1024,512]{1,0:T(8,128)(2,1)S(1)}, bf16[1024,512]{1,0:T(8,128)(2,1)}, u32[]{:S(2)}) copy-start(bf16[1024,512]{1,0:T(8,128)(2,1)} %param.20) | copy-start | bytes 3145732
  7.2 18.5 %all-gather.13.cloned.1.call-start = ((), (), s32[]{:S(2)}) async-start(), calls=%async_computation.12 | async-start | bytes 1572864 | tf_op jit(solution)/shard_map/all_gather | solution.py:169
  8.9 4.9 copy-start.79
  13.8 33.5 %all-gather.9.cloned.1.call-start = ((), (), s32[]{:S(2)}) async-start(), calls=%async_computation.8 | async-start | bytes 1572864 | tf_op jit(solution)/shard_map/all_gather | solution.py:169
  14.5 52.7 %reduce-scatter.13.cloned.1.call-start = ((), (), s32[]{:S(2)}) async-start(), calls=%async_computation.13 | async-start | bytes 3145728 | tf_op jit(solution)/shard_map/reduce_scatter | solution.py:180
  21.8 13.9 %copy-start.62 = (f32[512,32]{0,1:T(8,128)}, f32[512,32]{0,1:T(8,128)S(1)}, u32[]{:S(2)}) copy-start(f32[512,32]{0,1:T(8,128)S(1)} %get-tuple-element.259) | copy-start | bytes 196612
  21.8 13.9 %copy-start.64 = (f32[512,32]{0,1:T(8,128)}, f32[512,32]{0,1:T(8,128)S(1)}, u32[]{:S(2)}) copy-start(f32[512,32]{0,1:T(8,128)S(1)} %get-tuple-element.260) | copy-start | bytes 196612
  21.8 35.5 %copy-start.58 = (f32[512,32]{0,1:T(8,128)}, f32[512,32]{0,1:T(8,128)S(1)}, u32[]{:S(2)}) copy-start(f32[512,32]{0,1:T(8,128)S(1)} %get-tuple-element.253) | copy-start | bytes 196612
  21.8 35.5 %copy-start.60 = (f32[512,32]{0,1:T(8,128)}, f32[512,32]{0,1:T(8,128)S(1)}, u32[]{:S(2)}) copy-start(f32[512,32]{0,1:T(8,128)S(1)} %get-tuple-element.254) | copy-start | bytes 196612
  46.8 31.4 %reduce-scatter.9.cloned.1.call-start = ((), (), s32[]{:S(2)}) async-start(), calls=%async_computation.9 | async-start | bytes 3145728 | tf_op jit(solution)/shard_map/reduce_scatter | solution.py:180
  65.1 16.0 %copy-start.3 = (bf16[2,256,1024]{2,1,0:T(8,128)(2,1)S(1)}, bf16[2,256,1024]{2,1,0:T(8,128)(2,1)}, u32[]{:S(2)}) copy-start(bf16[2,256,1024]{2,1,0:T(8,128)(2,1)} %param.17) | copy-start | bytes 3145732
  65.1 16.0 %copy-start.82 = (f32[1024]{0:T(1024)S(1)}, f32[1024]{0:T(1024)}, u32[]{:S(2)}) copy-start(f32[1024]{0:T(1024)} %param.27) | copy-start | bytes 12292
  65.1 16.0 %copy-start.95 = (f32[1024]{0:T(1024)S(1)}, f32[1024]{0:T(1024)}, u32[]{:S(2)}) copy-start(f32[1024]{0:T(1024)} %param.28) | copy-start | bytes 12292
  67.2 28.9 %all-gather.15.cloned.1.call-start = ((), (), s32[]{:S(2)}) async-start(), calls=%async_computation.14 | async-start | bytes 1572864 | tf_op jit(solution)/shard_map/all_gather | solution.py:190
  79.6 4.8 copy-start.81
  79.6 4.8 copy-start.93
  85.8 30.8 %all-gather.11.cloned.1.call-start = ((), (), s32[]{:S(2)}) async-start(), calls=%async_computation.10 | async-start | bytes 1572864 | tf_op jit(solution)/shard_map/all_gather | solution.py:190
  86.3 50.1 %reduce-scatter.15.cloned.1.call-start = ((), (), s32[]{:S(2)}) async-start(), calls=%async_computation.15 | async-start | bytes 3145728 | tf_op jit(solution)/shard_map/reduce_scatter | solution.py:194
  96.1 16.2 %copy-start.97 = (bf16[2048,1024]{1,0:T(8,128)(2,1)S(1)}, bf16[2048,1024]{1,0:T(8,128)(2,1)}, u32[]{:S(2)}) copy-start(bf16[2048,1024]{1,0:T(8,128)(2,1)} %param.24) | copy-start | bytes 12582916
  116.0 31.2 %reduce-scatter.11.cloned.1.call-start = ((), (), s32[]{:S(2)}) async-start(), calls=%async_computation.11 | async-start | bytes 3145728 | tf_op jit(solution)/shard_map/reduce_scatter | solution.py:194
  116.5 16.2 %copy-start.98 = (bf16[2048,1024]{1,0:T(8,128)(2,1)S(1)}, bf16[2048,1024]{1,0:T(8,128)(2,1)}, u32[]{:S(2)}) copy-start(bf16[2048,1024]{1,0:T(8,128)(2,1)} %param.24) | copy-start | bytes 12582916
  136.3 14.0 %copy-start.84 = (f32[1024]{0:T(1024)S(1)}, f32[1024]{0:T(1024)}, u32[]{:S(2)}) copy-start(f32[1024]{0:T(1024)} %param.31) | copy-start | bytes 12292
  136.3 16.7 %copy-start.6 = (f32[256,1024]{1,0:T(8,128)S(1)}, f32[256,1024]{1,0:T(8,128)}, u32[]{:S(2)}) copy-start(f32[256,1024]{1,0:T(8,128)} %copy-done.5) | copy-start | bytes 3145732
  136.4 16.7 %copy-start.94 = (f32[1024]{0:T(1024)S(1)}, f32[1024]{0:T(1024)}, u32[]{:S(2)}) copy-start(f32[1024]{0:T(1024)} %param.32) | copy-start | bytes 12292
  136.4 30.1 %all-gather.21.cloned.1.call-start = ((), (), s32[]{:S(2)}) async-start(), calls=%async_computation.20 | async-start | bytes 1572864 | tf_op jit(solution)/shard_map/all_gather | solution.py:205
  148.6 4.4 copy-start.9
  148.6 4.4 copy-start.10
  148.6 4.4 copy-start.11
  156.1 24.0 %all-gather.17.cloned.1.call-start = ((), (), s32[]{:S(2)}) async-start(), calls=%async_computation.16 | async-start | bytes 1572864 | tf_op jit(solution)/shard_map/all_gather | solution.py:205
  158.3 43.2 %reduce-scatter.21.cloned.1.call-start = ((), (), s32[]{:S(2)}) async-start(), calls=%async_computation.21 | async-start | bytes 3145728 | tf_op jit(solution)/shard_map/reduce_scatter | solution.py:211
  166.5 9.9 %copy-start.99 = (bf16[1024,2048]{1,0:T(8,128)(2,1)S(1)}, bf16[1024,2048]{1,0:T(8,128)(2,1)}, u32[]{:S(2)}) copy-start(bf16[1024,2048]{1,0:T(8,128)(2,1)} %param.23) | copy-start | bytes 12582916
  180.1 25.8 %reduce-scatter.17.cloned.1.call-start = ((), (), s32[]{:S(2)}) async-start(), calls=%async_computation.17 | async-start | bytes 3145728 | tf_op jit(solution)/shard_map/reduce_scatter | solution.py:211
  180.1 9.9 %copy-start.100 = (bf16[1024,2048]{1,0:T(8,128)(2,1)S(1)}, bf16[1024,2048]{1,0:T(8,128)(2,1)}, u32[]{:S(2)}) copy-start(bf16[1024,2048]{1,0:T(8,128)(2,1)} %param.23) | copy-start | bytes 12582916
  190.0 4.0 copy-start.75
  193.7 36.9 %all-gather.23.cloned.1.call-start = ((), (), s32[]{:S(2)}) async-start(), calls=%async_computation.22 | async-start | bytes 1572864 | tf_op jit(solution)/shard_map/all_gather | solution.py:217
  213.9 35.5 %all-gather.19.cloned.1.call-start = ((), (), s32[]{:S(2)}) async-start(), calls=%async_computation.18 | async-start | bytes 1572864 | tf_op jit(solution)/shard_map/all_gather | solution.py:217
  214.0 9.6 copy-start.102
  214.0 9.6 copy-start.105
  223.5 5.7 copy-start.19
  230.2 61.7 %reduce-scatter.23.cloned.1.call-start = ((), (), s32[]{:S(2)}) async-start(), calls=%async_computation.23 | async-start | bytes 1572864 | tf_op jit(solution)/shard_map/reduce_scatter | solution.py:236
  232.6 5.5 slice-start.2
  232.7 6.1 slice-start.3
  249.1 42.8 %reduce-scatter.19.cloned.1.call-start = ((), (), s32[]{:S(2)}) async-start(), calls=%async_computation.19 | async-start | bytes 1572864 | tf_op jit(solution)/shard_map/reduce_scatter | solution.py:236
  251.3 5.5 slice-start
  251.4 6.2 slice-start.1
  268.0 10.2 %copy-start.25 = (bf16[8,64,512]{2,1,0:T(8,128)(2,1)S(1)}, bf16[8,64,512]{2,1,0:T(8,128)(2,1)}, u32[]{:S(2)}) copy-start(bf16[8,64,512]{2,1,0:T(8,128)(2,1)} %copy-done.24) | copy-start | bytes 1572868
  268.0 686.7 %all-reduce.5.cloned.1.call-start = ((), (), s32[]{:S(2)}) async-start(), calls=%async_computation.24 | async-start | bytes 50331648 | tf_op jit(solution)/shard_map/psum | solution.py:259
  268.2 9.9 %copy-start.38 = (bf16[512,1024]{1,0:T(8,128)(2,1)S(1)}, bf16[512,1024]{1,0:T(8,128)(2,1)}, u32[]{:S(2)}) copy-start(bf16[512,1024]{1,0:T(8,128)(2,1)} %all-gather.19.cloned.1.call-done) | copy-start | bytes 3145732
  268.3 10.7 %copy-start.36 = (bf16[8,64,512]{2,1,0:T(8,128)(2,1)S(1)}, bf16[8,64,512]{2,1,0:T(8,128)(2,1)}, u32[]{:S(2)}) copy-start(bf16[8,64,512]{2,1,0:T(8,128)(2,1)} %copy-done.35) | copy-start | bytes 1572868
  288.0 3.9 copy-start.78
  288.0 3.9 copy-start.80
  289.2 4.5 copy-start.92
  289.2 4.6 copy-start.90
  289.2 4.6 copy-start.86
  289.2 4.6 copy-start.88
  289.5 92.6 %copy-start.15 = (f32[256,1024]{1,0:T(8,128)S(1)}, f32[256,1024]{1,0:T(8,128)}, u32[]{:S(2)}) copy-start(f32[256,1024]{1,0:T(8,128)} %copy-done.14) | copy-start | bytes 3145732
  954.7 7.7 slice-start.6
  954.7 6.3 copy-start.34
  954.7 8.9 slice-start.7
  961.0 6.9 slice-start.4
  963.6 5.6 slice-start.5
  (67 other events, 141.3 us)
Sparse Core Ops, SparseCore 0:
  13.9 11.8 all-gather.12
  27.9 10.1 all-gather.8
  46.9 10.6 reduce-scatter.12
  67.3 10.8 reduce-scatter.8
  85.9 10.1 all-gather.14
  98.1 10.1 all-gather.10
  116.2 10.7 reduce-scatter.14
  136.5 10.7 reduce-scatter.10
  156.2 10.2 all-gather.20
  168.4 10.1 all-gather.16
  181.5 10.7 reduce-scatter.20
  195.1 10.7 reduce-scatter.16
  214.0 10.2 all-gather.22
  230.3 10.2 all-gather.18
  249.2 9.7 reduce-scatter.22
  268.1 9.7 reduce-scatter.18
  288.2 666.4 all-reduce.4
